TPU v7x, 32 devices: a whole 2x2x4 slice. The times are simulated.
32 devices in a mesh: orb: 16 (over z, x, core), grp: 2 (over y).
Axes of the slice: x: 2, y: 2, z: 4, core: 2. Of those that a mesh axis runs over, the one named last changes fastest.
Arguments:
- orbitals: float32 [512, 32, 1024], P('orb', 'grp'), may hold values from -6 to 6
- anchors: int32 [512], replicated, may hold values from 0 to 8
- wanted: int32 [16, 16, 2], replicated, may hold values from -1 to 511, as said below
- pairs: int32 [16, 2, 240, 2], P('orb'), may hold values from 0 to 511, as said below
- counts: int32 [16, 2], P('orb'), may hold values from 1 to 240, as said below
Outputs:
- exchange_field: float32 [512, 32, 1024], P('orb', 'grp')
Inputs may be any that keep to these rules, and one draw needn't show every extreme that they name: wanted[r, o] lists up to 2 different orbitals owned by group o (ids o * 32 to o * 32 + 31), -1 in empty slots; wanted[r, r] is empty; in every draw some pairs (r, o) fill all 2 slots. pairs[r, g, p] = (i, c) with i owned by group r and c below 64; a code below 32 never names i itself; pairs may repeat. `counts`: in each group r, one device g holds exactly 240 live pairs.
All inputs are finite; a program needn't handle non-finite values.
Results may differ from a plain program's by a relative error of at most 0.0085.
Values may be sent and summed in bfloat16 or wider, within the bound.
A program may use at most 128 MiB of HBM per device.

v0:
```python
import math

import jax
import jax.numpy as jnp
from jax import lax
from jax.sharding import PartitionSpec as P

screening = 0.01
block_pairs = 64


def sine_table(extent):
    ordinal = jnp.arange(extent, dtype=jnp.float32) + 1.0
    angles = math.pi * ordinal[:, None] * ordinal[None, :] / (extent + 1)
    return (math.sqrt(2.0 / (extent + 1)) * jnp.sin(angles)).astype(jnp.bfloat16)


def denominator(extent):
    ordinal = jnp.arange(extent, dtype=jnp.float32) + 1.0
    eigenvalue = 4.0 * jnp.sin(math.pi * ordinal / (2 * (extent + 1))) ** 2
    return (
        eigenvalue[:, None, None]
        + eigenvalue[None, :, None]
        + eigenvalue[None, None, :]
        + screening
    )


def selector(offset, extent, dtype):
    target_row = jnp.arange(extent, dtype=jnp.int32)[None, :, None]
    source_row = jnp.arange(extent, dtype=jnp.int32)[None, None, :]
    return (source_row == target_row - offset[:, None, None]).astype(dtype)


def potential(density, sine_rows, blocks, divisor):
    batch_size, extent, plane_size = density.shape

    def along_first(values):
        return jnp.einsum("kx,pxq->pkq", sine_rows, values, preferred_element_type=jnp.float32)

    def along_last(values):
        flat_rows = values.reshape(batch_size * extent * plane_size // 128, 128)
        product = jnp.dot(flat_rows, blocks, preferred_element_type=jnp.float32)
        return product.reshape(batch_size, extent, plane_size)

    def along_middle(values):
        cube = values.reshape(batch_size, extent, extent, extent)
        product = jnp.einsum("ky,pxyz->pxkz", sine_rows, cube, preferred_element_type=jnp.float32)
        return product.reshape(batch_size, extent, plane_size)

    section_one = along_first(density).astype(jnp.bfloat16)
    section_two = along_last(section_one).astype(jnp.bfloat16)
    section_three = (along_middle(section_two) / divisor).astype(jnp.bfloat16)
    section_four = along_middle(section_three).astype(jnp.bfloat16)
    section_five = along_last(section_four).astype(jnp.bfloat16)
    return along_first(section_five).astype(jnp.bfloat16)


def pair_terms(first_boxes, second_boxes, offset, sine_rows, blocks, divisor):
    extent = first_boxes.shape[1]
    forward = selector(offset, extent, jnp.bfloat16)
    shifted_box = jnp.einsum(
        "pxa,paq->pxq", forward, second_boxes, preferred_element_type=jnp.float32
    ).astype(jnp.bfloat16)
    density = (first_boxes.astype(jnp.float32) * shifted_box.astype(jnp.float32)).astype(
        jnp.bfloat16
    )
    field_wide = potential(density, sine_rows, blocks, divisor).astype(jnp.float32)
    own_term = field_wide * shifted_box.astype(jnp.float32)
    backward = selector(-offset, extent, jnp.float32)
    other_term = jnp.einsum(
        "pxa,paq->pxq",
        backward,
        field_wide * first_boxes.astype(jnp.float32),
        precision=lax.Precision.HIGHEST,
    )
    return (own_term, other_term)


def shards(orbitals, anchors, wanted, pairs, counts):
    group_size = lax.axis_size("grp")
    member = lax.axis_index("orb")
    position = lax.axis_index("grp")
    own_count = orbitals.shape[0]
    extent = orbitals.shape[1] * group_size
    plane_size = orbitals.shape[2]
    sine_rows = sine_table(extent)
    blocks = jnp.kron(jnp.eye(128 // extent, dtype=jnp.bfloat16), sine_rows)
    divisor = denominator(extent).reshape(extent, plane_size)
    slab_boxes = orbitals.astype(jnp.bfloat16)
    own_full = lax.all_gather(slab_boxes, "grp", axis=1, tiled=True)
    owner_rows = wanted.shape[0]
    per_owner = wanted.shape[2]
    slot_count = owner_rows * per_owner
    send_ids = lax.dynamic_index_in_dim(wanted, member, 1, keepdims=False).reshape(slot_count)
    send_live = send_ids >= 0
    send_local = jnp.where(send_live, send_ids - member * own_count, 0)
    outgoing = jnp.where(
        send_live[:, None, None], own_full[send_local], jnp.zeros((), jnp.bfloat16)
    )
    partner_full = lax.all_to_all(outgoing, "orb", split_axis=0, concat_axis=0, tiled=True)
    group_pairs = pairs[0]
    group_counts = counts[0]
    capacity = group_pairs.shape[1]
    flat_pairs = group_pairs.reshape(-1, 2)
    is_live = (jnp.arange(capacity, dtype=jnp.int32)[None, :] < group_counts[:, None]).reshape(-1)
    ranking = jnp.cumsum(is_live.astype(jnp.int32)) - 1
    is_mine = is_live & (ranking % group_size == position)
    target = jnp.where(is_mine, ranking // group_size, capacity)
    listed = jnp.zeros((capacity, 2), jnp.int32).at[target].set(flat_pairs, mode="drop")
    live_total = jnp.sum(is_mine.astype(jnp.int32))
    listed = jnp.concatenate([listed, jnp.zeros((block_pairs, 2), jnp.int32)], axis=0)
    first_ids = listed[:, 0]
    codes = listed[:, 1]
    request_rows = lax.dynamic_index_in_dim(wanted, member, 0, keepdims=False).reshape(slot_count)
    first_local = jnp.clip(first_ids - member * own_count, 0, own_count - 1)
    second_own = codes < own_count
    second_local = jnp.clip(codes, 0, own_count - 1)
    second_slot = jnp.clip(codes - own_count, 0, slot_count - 1)
    far_ids = request_rows[second_slot]
    second_ids = jnp.where(second_own, member * own_count + second_local, far_ids)
    valid = second_ids >= 0
    offsets = anchors[jnp.maximum(second_ids, 0)] - anchors[first_ids]

    def turn(turn_index, running):
        own_sum, partner_sum = running
        start_row = turn_index * block_pairs

        def window(values):
            return lax.dynamic_slice_in_dim(values, start_row, block_pairs, 0)

        in_range = (start_row + jnp.arange(block_pairs, dtype=jnp.int32) < live_total) & window(
            valid
        )
        from_own = window(second_own)
        first_boxes = own_full[window(first_local)]
        second_boxes = jnp.where(
            from_own[:, None, None],
            own_full[window(second_local)],
            partner_full[window(second_slot)],
        )
        own_term, other_term = pair_terms(
            first_boxes, second_boxes, window(offsets), sine_rows, blocks, divisor
        )
        own_sum = own_sum.at[jnp.where(in_range, window(first_local), own_count)].add(
            own_term, mode="drop"
        )
        own_sum = own_sum.at[jnp.where(in_range & from_own, window(second_local), own_count)].add(
            other_term, mode="drop"
        )
        partner_sum = partner_sum.at[
            jnp.where(in_range & ~from_own, window(second_slot), slot_count)
        ].add(other_term, mode="drop")
        return (own_sum, partner_sum)

    rounds = (live_total + block_pairs - 1) // block_pairs
    own_acc = jnp.zeros((own_count, extent, plane_size), jnp.float32)
    partner_acc = jnp.zeros((slot_count, extent, plane_size), jnp.float32)
    own_acc, partner_acc = lax.fori_loop(0, rounds, turn, (own_acc, partner_acc))
    returned = lax.all_to_all(
        partner_acc.astype(jnp.bfloat16), "orb", split_axis=0, concat_axis=0, tiled=True
    ).astype(partner_acc.dtype)
    own_acc = own_acc.at[jnp.where(send_live, send_local, own_count)].add(returned, mode="drop")
    result = lax.psum_scatter(
        own_acc.astype(jnp.bfloat16), "grp", scatter_dimension=1, tiled=True
    ).astype(jnp.float32)
    return result


def solution(mesh):
    return jax.shard_map(
        shards,
        mesh=mesh,
        in_specs=(P("orb", "grp", None), P(), P(), P("orb", None, None, None), P("orb", None)),
        out_specs=P("orb", "grp", None),
        check_vma=False,
    )
```

profile of v0, /device:TPU:0, one launch (start us, length us, event | category | flops | bytes accessed | tf_op | source)
XLA Modules:
  0.0 903.0 jit_solution(16073753513476197766)
XLA Ops:
  11.1 34.2 %all-gather.2.cloned.1.call-done = bf16[32,32,1024]{2,1,0:T(8,128)(2,1)} async-done(((bf16[32,16,1024]{2,1,0:T(8,128)(2,1)}), bf16[32,32,1024]{2,1,0:T(8,128)(2,1)}) %all-gather.2.cloned.1.call-update) | async-done | bytes 2097168 | tf_op jit(solution)/shard_map/all_gather | solution.py:91
  67.1 15.6 %select_select_fusion = s32[304]{0:T(512)S(1)} fusion(pred[304]{0:T(512)(128)(4,1)S(1)} %get-tuple-element.223, pred[304]{0:T(512)(128)(4,1)S(1)} %get-tuple-element.200, pred[304]{0:T(512)(128)(4,1)S(1)} %get-tuple-element.205, pred[304]{0:T(512)(128)(4,1)S(1)} %get-tuple-element.204, pred[304]{0:T(512)(128)(4,1)S(1)} %get-tuple-element.203, ...), kind=kLoop, calls=%fused_computation.131 | loop fusion | flops 7600 | bytes 10132 | tf_op jit(solution)/shard_map/gather | solution.py:120
  102.2 680.8 %while.14 = (s32[]{:T(128)}, f32[32,32,1024]{2,1,0:T(8,128)}, f32[32,32,1024]{2,1,0:T(8,128)}, s32[]{:T(128)}, s32[]{:T(128)}, /*index=5*/pred[304]{0:T(512)(128...) while((s32[]{:T(128)}, f32[32,32,1024]{2,1,0:T(8,128)}, ...), condition=%wide.region_8.9_spmd.clone.clone, body=%wide.region_4.8_spmd.clone.clone.sunk | while | flops 2596512512 | bytes 256338384 | solution.py:159
  140.1 18.7 %convert_element_type.238 = bf16[64,32,32,32]{3,2,1,0:T(8,128)(2,1)} reshape(bf16[16384,128]{1,0:T(8,128)(2,1)} %convolution_convert_fusion.5) | data formatting | bytes 8388608 | tf_op jit(solution)/shard_map/while/body/convert_element_type | solution.py:52
  158.9 27.1 %copy.21 = bf16[64,32,32,32]{0,2,3,1:T(8,128)(2,1)} copy(bf16[64,32,32,32]{3,2,1,0:T(8,128)(2,1)} %convert_element_type.238) | data formatting | bytes 8388608 | tf_op jit(solution)/shard_map/while/body/convert_element_type | solution.py:52
  186.1 9.9 %convert_bitcast_fusion.6 = bf16[64,32,32,32]{0,2,3,1:T(8,128)(2,1)} fusion(bf16[64,32,32,32]{0,2,3,1:T(8,128)(2,1)} %copy.21, f32[32,32,32]{1,2,0:T(8,128)S(1)} %add_add_fusion.2, f32[32]{0:T(128)S(1)} %get-tuple-element.517, f32[32]{0:T(128)S(1)} %get-tuple-element.518), kind=kOutput, calls=%fused_computation.25.clone.1 | convolution fusion | flops 274735104 | bytes 8519936 | tf_op jit(solution)/shard_map/while/body/ky,pxyz->pxkz/dot_general | solution.py:48
  195.9 29.2 %copy.22 = bf16[64,32,32,32]{3,2,1,0:T(8,128)(2,1)} copy(bf16[64,32,32,32]{0,2,3,1:T(8,128)(2,1)} %convert_bitcast_fusion.6) | data formatting | bytes 8388608 | tf_op jit(solution)/shard_map/while/body/convert_element_type | solution.py:54
  225.2 19.6 %convert_element_type.239 = bf16[16384,128]{1,0:T(8,128)(2,1)} reshape(bf16[64,32,32,32]{3,2,1,0:T(8,128)(2,1)} %copy.22) | data formatting | bytes 8388608 | tf_op jit(solution)/shard_map/while/body/convert_element_type | solution.py:54
  257.5 8.3 convert_multiply_fusion.7
  273.0 19.3 %scatter_fusion.2 = f32[32,32,1024]{2,1,0:T(8,128)} fusion(f32[32,32,1024]{2,1,0:T(8,128)} %get-tuple-element.483, s32[64]{0:T(128)S(1)} %get-tuple-element.457, f32[64,32,1024]{2,1,0:T(8,128)} %fusion.101), kind=kCustom, calls=%fused_computation.8.clone.clone.1 | custom fusion | flops 2097152 | bytes 25166080 | tf_op jit(solution)/shard_map/while/body/scatter-add | solution.py:153
  292.3 19.1 %scatter_fusion = f32[32,32,1024]{2,1,0:T(8,128)} fusion(f32[32,32,1024]{2,1,0:T(8,128)} %get-tuple-element.482, s32[64]{0:T(128)S(1)} %get-tuple-element.448, f32[64,32,1024]{2,1,0:T(8,128)} %get-tuple-element.453), kind=kCustom, calls=%fused_computation.6.clone.clone.1 | custom fusion | flops 2097152 | bytes 25166080 | tf_op jit(solution)/shard_map/while/body/scatter-add | solution.py:145
  311.4 18.6 %scatter_fusion.1 = f32[32,32,1024]{2,1,0:T(8,128)} fusion(f32[32,32,1024]{2,1,0:T(8,128)} %scatter_fusion, s32[64]{0:T(128)S(1)} %get-tuple-element.454, f32[64,32,1024]{2,1,0:T(8,128)} %fusion.101), kind=kCustom, calls=%fused_computation.7.clone.clone.1 | custom fusion | flops 2097152 | bytes 25166080 | tf_op jit(solution)/shard_map/while/body/scatter-add | solution.py:148
  367.9 18.7 %convert_element_type.238 = bf16[64,32,32,32]{3,2,1,0:T(8,128)(2,1)} reshape(bf16[16384,128]{1,0:T(8,128)(2,1)} %convolution_convert_fusion.5) | data formatting | bytes 8388608 | tf_op jit(solution)/shard_map/while/body/convert_element_type | solution.py:52
  386.7 27.1 %copy.21 = bf16[64,32,32,32]{0,2,3,1:T(8,128)(2,1)} copy(bf16[64,32,32,32]{3,2,1,0:T(8,128)(2,1)} %convert_element_type.238) | data formatting | bytes 8388608 | tf_op jit(solution)/shard_map/while/body/convert_element_type | solution.py:52
  413.9 9.8 %convert_bitcast_fusion.6 = bf16[64,32,32,32]{0,2,3,1:T(8,128)(2,1)} fusion(bf16[64,32,32,32]{0,2,3,1:T(8,128)(2,1)} %copy.21, f32[32,32,32]{1,2,0:T(8,128)S(1)} %add_add_fusion.2, f32[32]{0:T(128)S(1)} %get-tuple-element.517, f32[32]{0:T(128)S(1)} %get-tuple-element.518), kind=kOutput, calls=%fused_computation.25.clone.1 | convolution fusion | flops 274735104 | bytes 8519936 | tf_op jit(solution)/shard_map/while/body/ky,pxyz->pxkz/dot_general | solution.py:48
  423.7 29.2 %copy.22 = bf16[64,32,32,32]{3,2,1,0:T(8,128)(2,1)} copy(bf16[64,32,32,32]{0,2,3,1:T(8,128)(2,1)} %convert_bitcast_fusion.6) | data formatting | bytes 8388608 | tf_op jit(solution)/shard_map/while/body/convert_element_type | solution.py:54
  453.0 19.6 %convert_element_type.239 = bf16[16384,128]{1,0:T(8,128)(2,1)} reshape(bf16[64,32,32,32]{3,2,1,0:T(8,128)(2,1)} %copy.22) | data formatting | bytes 8388608 | tf_op jit(solution)/shard_map/while/body/convert_element_type | solution.py:54
  485.3 8.3 convert_multiply_fusion.7
  500.8 19.1 %scatter_fusion.2 = f32[32,32,1024]{2,1,0:T(8,128)} fusion(f32[32,32,1024]{2,1,0:T(8,128)} %get-tuple-element.483, s32[64]{0:T(128)S(1)} %get-tuple-element.457, f32[64,32,1024]{2,1,0:T(8,128)} %fusion.101), kind=kCustom, calls=%fused_computation.8.clone.clone.1 | custom fusion | flops 2097152 | bytes 25166080 | tf_op jit(solution)/shard_map/while/body/scatter-add | solution.py:153
  519.8 19.1 %scatter_fusion = f32[32,32,1024]{2,1,0:T(8,128)} fusion(f32[32,32,1024]{2,1,0:T(8,128)} %get-tuple-element.482, s32[64]{0:T(128)S(1)} %get-tuple-element.448, f32[64,32,1024]{2,1,0:T(8,128)} %get-tuple-element.453), kind=kCustom, calls=%fused_computation.6.clone.clone.1 | custom fusion | flops 2097152 | bytes 25166080 | tf_op jit(solution)/shard_map/while/body/scatter-add | solution.py:145
  538.9 18.4 %scatter_fusion.1 = f32[32,32,1024]{2,1,0:T(8,128)} fusion(f32[32,32,1024]{2,1,0:T(8,128)} %scatter_fusion, s32[64]{0:T(128)S(1)} %get-tuple-element.454, f32[64,32,1024]{2,1,0:T(8,128)} %fusion.101), kind=kCustom, calls=%fused_computation.7.clone.clone.1 | custom fusion | flops 2097152 | bytes 25166080 | tf_op jit(solution)/shard_map/while/body/scatter-add | solution.py:148
  595.3 18.7 %convert_element_type.238 = bf16[64,32,32,32]{3,2,1,0:T(8,128)(2,1)} reshape(bf16[16384,128]{1,0:T(8,128)(2,1)} %convolution_convert_fusion.5) | data formatting | bytes 8388608 | tf_op jit(solution)/shard_map/while/body/convert_element_type | solution.py:52
  614.0 27.1 %copy.21 = bf16[64,32,32,32]{0,2,3,1:T(8,128)(2,1)} copy(bf16[64,32,32,32]{3,2,1,0:T(8,128)(2,1)} %convert_element_type.238) | data formatting | bytes 8388608 | tf_op jit(solution)/shard_map/while/body/convert_element_type | solution.py:52
  641.2 9.8 %convert_bitcast_fusion.6 = bf16[64,32,32,32]{0,2,3,1:T(8,128)(2,1)} fusion(bf16[64,32,32,32]{0,2,3,1:T(8,128)(2,1)} %copy.21, f32[32,32,32]{1,2,0:T(8,128)S(1)} %add_add_fusion.2, f32[32]{0:T(128)S(1)} %get-tuple-element.517, f32[32]{0:T(128)S(1)} %get-tuple-element.518), kind=kOutput, calls=%fused_computation.25.clone.1 | convolution fusion | flops 274735104 | bytes 8519936 | tf_op jit(solution)/shard_map/while/body/ky,pxyz->pxkz/dot_general | solution.py:48
  651.1 29.2 %copy.22 = bf16[64,32,32,32]{3,2,1,0:T(8,128)(2,1)} copy(bf16[64,32,32,32]{0,2,3,1:T(8,128)(2,1)} %convert_bitcast_fusion.6) | data formatting | bytes 8388608 | tf_op jit(solution)/shard_map/while/body/convert_element_type | solution.py:54
  680.3 19.6 %convert_element_type.239 = bf16[16384,128]{1,0:T(8,128)(2,1)} reshape(bf16[64,32,32,32]{3,2,1,0:T(8,128)(2,1)} %copy.22) | data formatting | bytes 8388608 | tf_op jit(solution)/shard_map/while/body/convert_element_type | solution.py:54
  728.1 19.1 %scatter_fusion.2 = f32[32,32,1024]{2,1,0:T(8,128)} fusion(f32[32,32,1024]{2,1,0:T(8,128)} %get-tuple-element.483, s32[64]{0:T(128)S(1)} %get-tuple-element.457, f32[64,32,1024]{2,1,0:T(8,128)} %fusion.101), kind=kCustom, calls=%fused_computation.8.clone.clone.1 | custom fusion | flops 2097152 | bytes 25166080 | tf_op jit(solution)/shard_map/while/body/scatter-add | solution.py:153
  747.2 17.9 %scatter_fusion = f32[32,32,1024]{2,1,0:T(8,128)} fusion(f32[32,32,1024]{2,1,0:T(8,128)} %get-tuple-element.482, s32[64]{0:T(128)S(1)} %get-tuple-element.448, f32[64,32,1024]{2,1,0:T(8,128)} %get-tuple-element.453), kind=kCustom, calls=%fused_computation.6.clone.clone.1 | custom fusion | flops 2097152 | bytes 25166080 | tf_op jit(solution)/shard_map/while/body/scatter-add | solution.py:145
  765.1 17.6 %scatter_fusion.1 = f32[32,32,1024]{2,1,0:T(8,128)} fusion(f32[32,32,1024]{2,1,0:T(8,128)} %scatter_fusion, s32[64]{0:T(128)S(1)} %get-tuple-element.454, f32[64,32,1024]{2,1,0:T(8,128)} %fusion.101), kind=kCustom, calls=%fused_computation.7.clone.clone.1 | custom fusion | flops 2097152 | bytes 25166080 | tf_op jit(solution)/shard_map/while/body/scatter-add | solution.py:148
  785.5 60.1 %all_to_all.10 = bf16[32,32,1024]{2,1,0:T(8,128)(2,1)S(1)} all-to-all(bf16[32,32,1024]{2,1,0:T(8,128)(2,1)S(1)} %convert_element_type.112), channel_id=1, replica_groups=mesh['orb'=16,'grp'=2] {'orb'}, dimensions={0} | all-to-all | bytes 4194304 | tf_op jit(solution)/shard_map/all_to_all | solution.py:160
  848.1 9.6 %scatter_fusion.3 = f32[32,32,1024]{2,1,0:T(8,128)} fusion(f32[32,32,1024]{2,1,0:T(8,128)} %get-tuple-element.101, s32[32]{0:T(128)S(1)} %copy-done.9, f32[32,32,1024]{2,1,0:T(8,128)} %convert_element_type.113), kind=kCustom, calls=%fused_computation.10 | custom fusion | flops 1048576 | bytes 12583040 | tf_op jit(solution)/shard_map/scatter-add | solution.py:163
  861.5 31.9 %reduce-scatter.2.cloned.1.call-done = bf16[32,16,1024]{2,1,0:T(8,128)(2,1)} async-done(((bf16[32,32,1024]{2,1,0:T(8,128)(2,1)}), bf16[32,16,1024]{2,1,0:T(8,128)(2,1)}) %reduce-scatter.2.cloned.1.call-update) | async-done | bytes 1048592 | tf_op jit(solution)/shard_map/reduce_scatter | solution.py:164
  (150 shorter events, 238.6 us)
Async XLA Ops:
  6.5 76.5 %copy-start = (s32[512]{0:T(512)S(1)}, s32[512]{0:T(512)}, u32[]{:S(2)}) copy-start(s32[512]{0:T(512)} %param.8) | copy-start | bytes 6148
  6.5 2.8 copy-start.5
  6.5 38.8 %all-gather.2.cloned.1.call-start = ((), (), s32[]{:S(2)}) async-start(), calls=%async_computation.3 | async-start | bytes 3145728 | tf_op jit(solution)/shard_map/all_gather | solution.py:91
  47.6 7.2 copy-start.10
  47.6 9.5 %copy-start.8 = (s32[1,2,240,2]{2,3,1,0:T(2,128)S(1)}, s32[1,2,240,2]{2,3,1,0:T(2,128)}, u32[]{:S(2)}) copy-start(s32[1,2,240,2]{2,3,1,0:T(2,128)} %param.10) | copy-start | bytes 11524
  49.1 46.7 %all-to-all-start = ((bf16[32,32,1024]{2,1,0:T(8,128)(2,1)}), bf16[32,32,1024]{2,1,0:T(8,128)(2,1)S(1)}, u32[]{:S(2)}, u32[]{:S(2)}) async-start(bf16[32,32,1024]{2,1,0:T(8,128)(2,1)} %broadcast_select_fusion), calls=%async_computation | async-start | bytes 4194304 | tf_op jit(solution)/shard_map/all_to_all | solution.py:101
  54.8 838.7 %reduce-scatter.2.cloned.1.call-start = ((), (), s32[]{:S(2)}) async-start(), calls=%async_computation.4 | async-start | bytes 3145728 | tf_op jit(solution)/shard_map/reduce_scatter | solution.py:164
  95.9 1.3 copy-start.4
  97.2 5.0 copy-start.3
  102.2 0.5 copy-start.6
  158.9 27.1 %copy-start.7 = (f32[32]{0:T(128)S(1)}, f32[32]{0:T(128)}, u32[]{:S(2)}) copy-start(f32[32]{0:T(128)} %copy-done.6) | copy-start | bytes 388 | tf_op jit(solution)/shard_map/while
  257.5 8.4 copy-start.2
  330.0 0.5 copy-start.6
  386.7 27.1 %copy-start.7 = (f32[32]{0:T(128)S(1)}, f32[32]{0:T(128)}, u32[]{:S(2)}) copy-start(f32[32]{0:T(128)} %copy-done.6) | copy-start | bytes 388 | tf_op jit(solution)/shard_map/while
  485.3 8.4 copy-start.2
  557.4 0.5 copy-start.6
  614.0 27.1 %copy-start.7 = (f32[32]{0:T(128)S(1)}, f32[32]{0:T(128)}, u32[]{:S(2)}) copy-start(f32[32]{0:T(128)} %copy-done.6) | copy-start | bytes 388 | tf_op jit(solution)/shard_map/while
  712.7 8.4 copy-start.2
  845.6 2.5 copy-start.9
  857.7 38.5 %copy-start.1 = (s32[512]{0:T(512)S(1)}, s32[512]{0:T(512)}, u32[]{:S(2)}) copy-start(s32[512]{0:T(512)} %param.8) | copy-start | bytes 6148
Sparse Core Ops, SparseCore 0:
  9.4 35.8 all-gather.1
  861.7 31.6 reduce-scatter.1
where the time goes:
time: 908 us; the launch traced here: 903 us
  local copies, waits for them, and re-layouts  377 us (42%)
  other arithmetic  223 us (25%)
  matrix products  149 us (16%)
  waiting for transfers between devices  73.5 us (8%)
  blocking collectives  60.1 us (7%)
  between operations  14.3 us (2%)
    convert_element_type x6, local copies, waits for them, and re-layouts, potential(): section_four = along_middle(section_three).astype(jnp.bfloat16)  147 us
    convert_element_type x6, local copies, waits for them, and re-layouts, potential(): section_two = along_last(section_one).astype(jnp.bfloat16)  137 us
    all_to_all x1, blocking collectives, shards(): lax.all_to_all(partner_acc.astype(jnp.bfloat16), 'orb', split_axis=0, con...  60.1 us
    scatter-add x3, other arithmetic, turn(): partner_sum = partner_sum.at[jnp.where(in_range & ~from_own, window(secon...  57.5 us
    scatter-add x3, other arithmetic, turn(): own_sum.at[jnp.where(in_range, window(first_local), own_count)]  56.2 us
    scatter-add x3, other arithmetic, turn(): own_sum.at[jnp.where(in_range & from_own, window(second_local), own_count)]  54.6 us
    dot_general x6, matrix products, along_first(): jnp.einsum('kx,pxq->pkq', sine_rows, values, preferred_element_type=jnp.f...  45.5 us
    all_gather x1, waiting for transfers between devices, shards(): own_full = lax.all_gather(slab_boxes, 'grp', axis=1, tiled=True)  34.2 us
  transfers between devices with their start and end apart: 3, of which 3 were waited for; matrix products, arithmetic and copies ran while one was open for 4% of the time, Pallas kernels for 0%

commit v1 on v0

v1 whole, which is shorter than its diff:
```python
import functools
import math

import jax
import jax.numpy as jnp
from jax import lax
from jax.experimental import pallas as pl
from jax.experimental.pallas import tpu as pltpu
from jax.sharding import PartitionSpec as P

screening = 0.01
batch = 8
lanes = 128


def sine_table(extent):
    ordinal = jnp.arange(extent, dtype=jnp.float32) + 1.0
    angles = math.pi * ordinal[:, None] * ordinal[None, :] / (extent + 1)
    return (math.sqrt(2.0 / (extent + 1)) * jnp.sin(angles)).astype(jnp.bfloat16)


def denominator(extent):
    ordinal = jnp.arange(extent, dtype=jnp.float32) + 1.0
    eigenvalue = 4.0 * jnp.sin(math.pi * ordinal / (2 * (extent + 1))) ** 2
    return (
        eigenvalue[:, None, None]
        + eigenvalue[None, :, None]
        + eigenvalue[None, None, :]
        + screening
    )


def list_kernel(sizes, where, pairs, counts, anchors, request, listed, total, spare, tally):
    group_size, capacity, own_count, per_owner, per, slots, pad = sizes
    member, position = where[0], where[1]
    dead = own_count + slots

    def pack(first, second, offset):
        return first + second * 256 + (offset + pad) * 65536

    for g in range(group_size):
        tally[g] = 0

    def scan(g, p, state):
        mine, own = state
        at = (g * capacity + p) * 2
        first_id, code = pairs[at], pairs[at + 1]
        first = jnp.clip(first_id - member * own_count, 0, own_count - 1)
        is_own = code < own_count
        slot = jnp.clip(code - own_count, 0, request.shape[0] - 1)
        second_id = jnp.where(is_own, member * own_count + code, request[slot])
        valid = second_id >= 0
        offset = anchors[jnp.maximum(second_id, 0)] - anchors[first_id]
        offset = jnp.clip(offset, -pad, pad)
        owner, sub = slot // per_owner, slot % per_owner
        if group_size <= per_owner:
            holder, local = sub // per, owner * per + sub % per
        else:
            holder, local = sub + per_owner * (owner % (group_size // per_owner)), owner

        here = jnp.logical_and(valid, jnp.logical_and(~is_own, holder == position))
        listed[mine] = pack(first, own_count + local, offset)
        spare[own] = pack(first, jnp.clip(code, 0, own_count - 1), offset)
        far = jnp.where(jnp.logical_and(valid, ~is_own), 1, 0)
        tally[holder] = tally[holder] + far
        return (
            mine + jnp.where(here, 1, 0),
            own + jnp.where(is_own, 1, 0),
        )

    state = (jnp.int32(0), jnp.int32(0))
    for g in range(group_size):
        state = lax.fori_loop(0, counts[g], functools.partial(scan, g), state)
    mine, own = state
    everything = own
    for g in range(group_size):
        everything = everything + tally[g]
    share = (everything + group_size - 1) // group_size
    begin = jnp.int32(0)
    for g in range(group_size):
        begin = begin + jnp.where(g < position, jnp.maximum(share - tally[g], 0), 0)
    stop = jnp.minimum(begin + jnp.maximum(share - mine, 0), own)
    begin = jnp.minimum(begin, own)

    def take(i, count):
        listed[count] = spare[i]
        return count + 1

    mine = lax.fori_loop(begin, stop, take, mine)
    for i in range(batch):
        listed[mine + i] = pack(dead, dead, 0)
    total[0] = mine


def pair_kernel(
    sizes, listed, total, own, far, plane, first_block, scale, own_out, far_out,
    boxes, sums, density, middle, field,
):
    own_count, slots, extent, width, pad = sizes
    chunks = width // lanes
    tall = extent + 2 * pad
    dead = own_count + slots
    inner = slice(pad, pad + extent)
    zeros = jnp.zeros((tall, lanes), jnp.float32)
    edge = jnp.zeros((pad, lanes), jnp.float32)

    def clear(n, carry):
        for s in range(chunks):
            sums[n, s] = zeros
        return carry

    lax.fori_loop(0, dead + 1, clear, 0)

    def fill(source, base, n, carry):
        for s in range(chunks):
            boxes[base + n, s, :pad] = edge
            boxes[base + n, s, inner] = source[n, :, s * lanes : (s + 1) * lanes].astype(jnp.float32)
            boxes[base + n, s, pad + extent :] = edge
        return carry

    lax.fori_loop(0, own_count, functools.partial(fill, own, 0), 0)
    lax.fori_loop(0, slots, functools.partial(fill, far, own_count), 0)
    for s in range(chunks):
        boxes[dead, s] = zeros

    def unpack(turn, b):
        word = listed[turn * batch + b]
        first, second = word % 256, (word // 256) % 256
        return first, second, 2 * pad - word // 65536

    step = 256

    def turn_body(turn, carry):
        for b in range(batch):
            first, second, start = unpack(turn, b)
            rows = slice(b * extent, (b + 1) * extent)
            for s in range(chunks):
                moved = boxes[second, s, pl.ds(start, extent), :]
                product = boxes[first, s, inner] * moved
                density[rows, s * lanes : (s + 1) * lanes] = product.astype(jnp.bfloat16)
        for n in range(width // step):
            columns = slice(n * step, (n + 1) * step)
            wave = jnp.dot(density[...], plane[:, columns], preferred_element_type=jnp.float32)
            wave = jnp.dot(
                first_block[...], wave.astype(jnp.bfloat16), preferred_element_type=jnp.float32
            )
            wave = wave.reshape(batch, extent, step) * scale[:, columns][None]
            wave = wave.reshape(batch * extent, step).astype(jnp.bfloat16)
            wave = jnp.dot(first_block[...], wave, preferred_element_type=jnp.float32)
            middle[:, columns] = wave.astype(jnp.bfloat16)
        for n in range(width // step):
            columns = slice(n * step, (n + 1) * step)
            field[:, columns] = jnp.dot(
                middle[...], plane[:, columns], preferred_element_type=jnp.float32
            )
        for b in range(batch):
            first, second, start = unpack(turn, b)
            rows = slice(b * extent, (b + 1) * extent)
            for s in range(chunks):
                moved = boxes[second, s, pl.ds(start, extent), :]
                own_box = boxes[first, s, inner]
                value = field[rows, s * lanes : (s + 1) * lanes]
                sums[first, s, inner] += value * moved
                sums[second, s, pl.ds(start, extent), :] += value * own_box
        return carry

    lax.fori_loop(0, (total[0] + batch - 1) // batch, turn_body, 0)

    def give(target, base, n, carry):
        for s in range(chunks):
            target[n, :, s * lanes : (s + 1) * lanes] = sums[base + n, s, inner].astype(target.dtype)
        return carry

    lax.fori_loop(0, own_count, functools.partial(give, own_out, 0), 0)
    lax.fori_loop(0, slots, functools.partial(give, far_out, own_count), 0)


def join_kernel(local, own, returned, out, total):
    total[...] = own[...]

    def add(n, carry):
        total[local[n]] += returned[n].astype(jnp.float32)
        return carry

    lax.fori_loop(0, returned.shape[0], add, 0)
    out[...] = total[...].astype(out.dtype)


def shards(orbitals, anchors, wanted, pairs, counts):
    group_size = lax.axis_size("grp")
    member = lax.axis_index("orb")
    position = lax.axis_index("grp")
    own_count = orbitals.shape[0]
    extent = orbitals.shape[1] * group_size
    width = orbitals.shape[2]
    pad = extent // 4
    owners, per_owner = wanted.shape[0], wanted.shape[2]
    per = -(-per_owner // group_size)
    slots = owners * per
    capacity = pairs.shape[2]
    smem = pl.BlockSpec(memory_space=pltpu.SMEM)
    vmem = pl.BlockSpec(memory_space=pltpu.VMEM)

    own_full = lax.all_gather(orbitals.astype(jnp.bfloat16), "grp", axis=1, tiled=True)

    sine_rows = sine_table(extent)
    plane = jnp.kron(sine_rows, sine_rows)
    first_block = jnp.kron(jnp.eye(batch, dtype=jnp.bfloat16), sine_rows)
    scale = (1.0 / denominator(extent)).reshape(extent, width)

    send_ids = lax.dynamic_index_in_dim(wanted, member, 1, keepdims=False)
    request = lax.dynamic_index_in_dim(wanted, member, 0, keepdims=False).reshape(-1)
    if group_size <= per_owner:
        send_ids = jnp.pad(send_ids, ((0, 0), (0, per * group_size - per_owner)), constant_values=-1)
        start = position * per
    else:
        start = position % per_owner
    send_ids = lax.dynamic_slice_in_dim(send_ids, start, per, 1).reshape(slots)
    send_local = jnp.where(send_ids >= 0, send_ids - member * own_count, 0)

    size = group_size * capacity + 2 * batch
    sizes = (group_size, capacity, own_count, per_owner, per, slots, pad)
    listed, total = pl.pallas_call(
        functools.partial(list_kernel, sizes),
        out_shape=(
            jax.ShapeDtypeStruct((size,), jnp.int32),
            jax.ShapeDtypeStruct((1,), jnp.int32),
        ),
        in_specs=[smem] * 5,
        out_specs=(smem, smem),
        scratch_shapes=[pltpu.SMEM((size,), jnp.int32), pltpu.SMEM((group_size,), jnp.int32)],
    )(
        jnp.stack([member, position]).astype(jnp.int32),
        pairs.reshape(-1),
        counts.reshape(-1),
        anchors,
        request,
    )

    far_full = lax.all_to_all(own_full[send_local], "orb", split_axis=0, concat_axis=0, tiled=True)

    tall = extent + 2 * pad
    chunks = width // lanes
    kept = own_count + slots + 1
    own_sum, far_sum = pl.pallas_call(
        functools.partial(pair_kernel, (own_count, slots, extent, width, pad)),
        out_shape=(
            jax.ShapeDtypeStruct((own_count, extent, width), jnp.float32),
            jax.ShapeDtypeStruct((slots, extent, width), jnp.bfloat16),
        ),
        in_specs=[smem, smem] + [vmem] * 5,
        out_specs=(vmem, vmem),
        scratch_shapes=[
            pltpu.VMEM((kept, chunks, tall, lanes), jnp.float32),
            pltpu.VMEM((kept, chunks, tall, lanes), jnp.float32),
            pltpu.VMEM((batch * extent, width), jnp.bfloat16),
            pltpu.VMEM((batch * extent, width), jnp.bfloat16),
            pltpu.VMEM((batch * extent, width), jnp.float32),
        ],
        compiler_params=pltpu.CompilerParams(vmem_limit_bytes=56 * 2**20),
    )(listed, total, own_full, far_full, plane, first_block, scale)

    returned = lax.all_to_all(far_sum, "orb", split_axis=0, concat_axis=0, tiled=True)
    joined = pl.pallas_call(
        join_kernel,
        out_shape=jax.ShapeDtypeStruct((own_count, extent, width), jnp.bfloat16),
        in_specs=[smem, vmem, vmem],
        out_specs=vmem,
        scratch_shapes=[pltpu.VMEM((own_count, extent, width), jnp.float32)],
        compiler_params=pltpu.CompilerParams(vmem_limit_bytes=40 * 2**20),
    )(send_local, own_sum, returned)
    return lax.psum_scatter(joined, "grp", scatter_dimension=1, tiled=True).astype(jnp.float32)


def solution(mesh):
    return jax.shard_map(
        shards,
        mesh=mesh,
        in_specs=(P("orb", "grp", None), P(), P(), P("orb", None, None, None), P("orb", None)),
        out_specs=P("orb", "grp", None),
        check_vma=False,
    )
```

time: 908 us -> 243 us (0.27)
  local copies, waits for them, and re-layouts: 377 us -> 21.9 us
  other arithmetic: 223 us -> 11.5 us
  matrix products: 149 us -> 0 us
  Pallas kernels: 0 us -> 94.1 us
  blocking collectives: 60.1 us -> 30.9 us
    convert_element_type x15 -> x0, local copies, waits for them, and re-layouts: 306 us -> none  [the longest x6 147 us: potential(): section_four = along_middle(section_three).astype(jnp.bfloat16)]
    scatter-add x10 -> x0, other arithmetic: 178 us -> none  [the longest x3 57.5 us: turn(): partner_sum = partner_sum.at[jnp.where(in_range & ~from_own, window(secon...]
    dot_general x21 -> x0, matrix products: 149 us -> none  [the longest x6 45.5 us: along_first(): jnp.einsum('kx,pxq->pkq', sine_rows, values, preferred_element_type=jnp.f...]
    pallas_call x0 -> x3, Pallas kernels: none -> 94.1 us  [the longest x1 81.4 us: shards(): pl.pallas_call(functools.partial(pair_kernel, (own_count, slots, extent,...]
    gather x13 -> x0, local copies, waits for them, and re-layouts: 36.2 us -> none  [the longest x3 13.2 us: turn(): partner_full[window(second_slot)]]
    all_to_all x1, blocking collectives: 60.1 us -> 30.9 us  [shards(): lax.all_to_all(far_sum, 'orb', split_axis=0, concat_axis=0, tiled=True)]
    reshape x4 -> x2, local copies, waits for them, and re-layouts: 21.9 us -> 1.4 us  [the longest x1 0.74 us: shards(): pairs.reshape(-1)]
    gather x14 -> x0, other arithmetic: 17.6 us -> none  [the longest x3 17.5 us: shards(): far_ids = request_rows[second_slot]]
  transfers between devices with their start and end apart: 3 -> 3, of which waited for: 3 -> 2; matrix products, arithmetic and copies ran while one was open for 4% -> 9% of each run, Pallas kernels for 0% -> 4%
where the time goes in v1:
time: 243 us
  Pallas kernels  94.1 us (39%)
  waiting for transfers between devices  65.3 us (27%)
  blocking collectives  30.9 us (13%)
  local copies, waits for them, and re-layouts  21.9 us (9%)
  between operations  13.5 us (6%)
  other arithmetic  11.5 us (5%)
  starting transfers between devices  5.66 us (2%)
    pallas_call x1, Pallas kernels, shards(): pl.pallas_call(functools.partial(pair_kernel, (own_count, slots, extent,...  81.4 us
    all_gather x1, waiting for transfers between devices, shards(): lax.all_gather(orbitals.astype(jnp.bfloat16), 'grp', axis=1, tiled=True)  33.8 us
    reduce_scatter x1, waiting for transfers between devices, shards(): lax.psum_scatter(joined, 'grp', scatter_dimension=1, tiled=True)  31.4 us
    all_to_all x1, blocking collectives, shards(): lax.all_to_all(far_sum, 'orb', split_axis=0, concat_axis=0, tiled=True)  30.9 us
    mul x1, local copies, waits for them, and re-layouts, shards(): plane = jnp.kron(sine_rows, sine_rows)  12.4 us
    pallas_call x1, Pallas kernels, shards(): pl.pallas_call(functools.partial(list_kernel, sizes), out_shape=(jax.Shap...  10.1 us
    all_to_all x1, starting transfers between devices, shards(): lax.all_to_all(own_full[send_local], 'orb', split_axis=0, concat_axis=0,...  5.61 us
  transfers between devices with their start and end apart: 3, of which 2 were waited for; matrix products, arithmetic and copies ran while one was open for 9% of the time, Pallas kernels for 4%

profile of v1, /device:TPU:0, one launch (start us, length us, event | category | flops | bytes accessed | tf_op | source)
XLA Modules:
  0.0 242.8 jit_solution(15617981054632694397)
XLA Ops:
  6.5 2.8 %convert_element_type.26 = bf16[32,16,1024]{2,1,0:T(8,128)(2,1)} convert(f32[32,16,1024]{2,1,0:T(8,128)} %param.5) | non-fusion elementwise | flops 524288 | bytes 3145728 | tf_op jit(solution)/shard_map/convert_element_type | solution.py:204
  9.3 0.0 all-gather.2.cloned.1.call-update
  9.4 0.1 copy.8
  9.4 0.7 reshape.205.request
  10.1 0.1 copy.7
  10.2 0.7 reshape.203.pairs
  11.0 0.4 fusion.local
  11.5 33.8 %all-gather.2.cloned.1.call-done.own = bf16[32,32,1024]{2,1,0:T(8,128)(2,1)} async-done(((bf16[32,16,1024]{2,1,0:T(8,128)(2,1)}), bf16[32,32,1024]{2,1,0:T(8,128)(2,1)}) %all-gather.2.cloned.1.call-update) | async-done | bytes 2097168 | tf_op jit(solution)/shard_map/all_gather | solution.py:204
  45.3 3.2 %gather_fusion = bf16[16,32,1024]{2,1,0:T(8,128)(2,1)} fusion(bf16[32,32,1024]{2,1,0:T(8,128)(2,1)} %all-gather.2.cloned.1.call-done.own, s32[1024]{0:T(1024)S(1)} %pad_clamp_fusion), kind=kCustom, calls=%fused_computation | custom fusion | bytes 2097216 | tf_op jit(solution)/shard_map/gather | solution.py:240
  48.5 5.6 %all-to-all-start = ((bf16[16,32,1024]{2,1,0:T(8,128)(2,1)}), bf16[16,32,1024]{2,1,0:T(8,128)(2,1)S(1)}, u32[]{:S(2)}, u32[]{:S(2)}) async-start(bf16[16,32,1024]{2,1,0:T(8,128)(2,1)} %gather_fusion), calls=%async_computation | async-start | bytes 2097152 | tf_op jit(solution)/shard_map/all_to_all | solution.py:240
  54.1 0.0 reduce-scatter.2.cloned.1.call-start
  54.2 0.1 multiply_convert_fusion
  54.3 3.8 %broadcast_multiply_fusion = bf16[32,32,32,32]{3,2,1,0:T(8,128)(2,1)} fusion(bf16[32,32]{1,0:T(8,128)(2,1)S(1)} %multiply_convert_fusion), kind=kLoop, calls=%fused_computation.1 | loop fusion | flops 1048576 | bytes 2099200 | tf_op jit(solution)/shard_map/jit(kron)/mul | solution.py:207
  58.1 12.4 %mul.141.plane = bf16[1024,1024]{1,0:T(8,128)(2,1)} reshape(bf16[32,32,32,32]{3,2,1,0:T(8,128)(2,1)} %broadcast_multiply_fusion) | data formatting | bytes 4194304 | tf_op jit(solution)/shard_map/jit(kron)/mul | solution.py:207
  70.5 0.1 broadcast_multiply_fusion.1
  70.7 1.0 mul.145.first_block
  71.7 0.1 broadcast_add_fusion
  71.8 0.2 add.102
  72.0 0.2 add.103
  72.3 0.1 add.104
  72.3 0.6 pad_add_fusion.where
  72.9 10.1 %shard_map.55 = (s32[496]{0:T(512)}, s32[1]{0:T(128)}) custom-call(s32[2]{0:T(128)} %pad_add_fusion.where, s32[960]{0:T(1024)} %reshape.203.pairs, s32[2]{0:T(128)} %bitcast.13, s32[512]{0:T(512)} %anchors.1, s32[32]{0:T(128)} %reshape.205.request), custom_call_target="tpu_custom_call" | custom-call | tf_op jit(solution)/shard_map/pallas_call | solution.py:223
  83.1 0.7 add_divide_fusion.scale
  83.7 0.0 all-to-all-done.far
  83.7 1.0 copy-done.1
  84.7 81.4 %shard_map.56 = (f32[32,32,1024]{2,1,0:T(8,128)}, bf16[16,32,1024]{2,1,0:T(8,128)(2,1)}) custom-call(s32[496]{0:T(512)} %get-tuple-element.9.listed, s32[1]{0:T(128)} %get-tuple-element.10.total, bf16[32,32,1024]{2,1,0:T(8,128)(2,1)} %all-gather.2.cloned.1.call-done.own, bf16[16,32,1024]{2,1,0:T(8,128)(2,1)} %copy-done.1, bf16[1024,1024]{1,0:T(8,128)(2,1)} %mul.141.plane, ...), custom_call_target="tpu_custom_call" | custom-call | tf_op jit(solution)/shard_map/pallas_call | solution.py:245
  166.1 30.9 %all_to_all.10.returned = bf16[16,32,1024]{2,1,0:T(8,128)(2,1)S(1)} all-to-all(bf16[16,32,1024]{2,1,0:T(8,128)(2,1)} %get-tuple-element.12), channel_id=1, replica_groups=mesh['orb'=16,'grp'=2] {'orb'}, dimensions={0} | all-to-all | bytes 2097152 | tf_op jit(solution)/shard_map/all_to_all | solution.py:263
  197.0 2.2 copy-done
  199.2 2.6 %shard_map.57 = bf16[32,32,1024]{2,1,0:T(8,128)(2,1)} custom-call(s32[16]{0:T(128)S(1)} %fusion.local, f32[32,32,1024]{2,1,0:T(8,128)S(1)} %copy-done, bf16[16,32,1024]{2,1,0:T(8,128)(2,1)S(1)} %all_to_all.10.returned), custom_call_target="tpu_custom_call" | custom-call | tf_op jit(solution)/shard_map/pallas_call | solution.py:264
  201.8 0.0 reduce-scatter.2.cloned.1.call-update
  201.8 31.4 %reduce-scatter.2.cloned.1.call-done = bf16[32,16,1024]{2,1,0:T(8,128)(2,1)} async-done(((bf16[32,32,1024]{2,1,0:T(8,128)(2,1)}), bf16[32,16,1024]{2,1,0:T(8,128)(2,1)}) %reduce-scatter.2.cloned.1.call-update) | async-done | bytes 1048592 | tf_op jit(solution)/shard_map/reduce_scatter | solution.py:272
  233.2 2.8 %convert_element_type.29 = f32[32,16,1024]{2,1,0:T(8,128)} convert(bf16[32,16,1024]{2,1,0:T(8,128)(2,1)} %reduce-scatter.2.cloned.1.call-done) | non-fusion elementwise | flops 524288 | bytes 3145728 | tf_op jit(solution)/shard_map/convert_element_type | solution.py:272
  (14 shorter events, 0.1 us)
Async XLA Ops:
  6.5 2.8 %copy-start.2 = (s32[16,16,2]{1,2,0:T(2,128)S(1)}, s32[16,16,2]{1,2,0:T(2,128)}, u32[]{:S(2)}) copy-start(s32[16,16,2]{1,2,0:T(2,128)} %param.7) | copy-start | bytes 6148
  6.5 3.6 %copy-start.3 = (s32[1,2,240,2]{2,3,1,0:T(2,128)S(1)}, s32[1,2,240,2]{2,3,1,0:T(2,128)}, u32[]{:S(2)}) copy-start(s32[1,2,240,2]{2,3,1,0:T(2,128)} %param.8) | copy-start | bytes 11524
  6.5 38.8 %all-gather.2.cloned.1.call-start = ((), (), s32[]{:S(2)}) async-start(), calls=%async_computation.3 | async-start | bytes 3145728 | tf_op jit(solution)/shard_map/all_gather | solution.py:204
  48.5 35.3 %all-to-all-start = ((bf16[16,32,1024]{2,1,0:T(8,128)(2,1)}), bf16[16,32,1024]{2,1,0:T(8,128)(2,1)S(1)}, u32[]{:S(2)}, u32[]{:S(2)}) async-start(bf16[16,32,1024]{2,1,0:T(8,128)(2,1)} %gather_fusion), calls=%async_computation | async-start | bytes 2097152 | tf_op jit(solution)/shard_map/all_to_all | solution.py:240
  54.1 179.1 %reduce-scatter.2.cloned.1.call-start = ((), (), s32[]{:S(2)}) async-start(), calls=%async_computation.4 | async-start | bytes 3145728 | tf_op jit(solution)/shard_map/reduce_scatter | solution.py:272
  83.7 1.0 copy-start.1
  197.0 2.2 copy-start
Sparse Core Ops, SparseCore 0:
  9.4 35.8 all-gather.1
  201.9 31.2 reduce-scatter.1

commit v2 on v1

v2 whole, which is shorter than its diff:
```python
import functools
import math

import jax
import jax.numpy as jnp
from jax import lax
from jax.experimental import pallas as pl
from jax.experimental.pallas import tpu as pltpu
from jax.sharding import PartitionSpec as P

screening = 0.01
batch = 8
lanes = 128


def sine_table(extent):
    ordinal = jnp.arange(extent, dtype=jnp.float32) + 1.0
    angles = math.pi * ordinal[:, None] * ordinal[None, :] / (extent + 1)
    return (math.sqrt(2.0 / (extent + 1)) * jnp.sin(angles)).astype(jnp.bfloat16)


def denominator(extent):
    ordinal = jnp.arange(extent, dtype=jnp.float32) + 1.0
    eigenvalue = 4.0 * jnp.sin(math.pi * ordinal / (2 * (extent + 1))) ** 2
    return (
        eigenvalue[:, None, None]
        + eigenvalue[None, :, None]
        + eigenvalue[None, None, :]
        + screening
    )


def list_kernel(
    sizes, where, pairs, counts, anchors, request, far_list, own_list, totals, spare, tally
):
    group_size, capacity, own_count, per_owner, per, slots, pad = sizes
    member, position = where[0], where[1]

    def pack(first, second, offset):
        return first + second * 256 + (offset + pad) * 65536

    for g in range(group_size):
        tally[g] = 0

    def scan(g, p, state):
        mine, own = state
        at = (g * capacity + p) * 2
        first_id, code = pairs[at], pairs[at + 1]
        first = jnp.clip(first_id - member * own_count, 0, own_count - 1)
        is_own = code < own_count
        slot = jnp.clip(code - own_count, 0, request.shape[0] - 1)
        second_id = jnp.where(is_own, member * own_count + code, request[slot])
        valid = second_id >= 0
        offset = anchors[jnp.maximum(second_id, 0)] - anchors[first_id]
        offset = jnp.clip(offset, -pad, pad)
        owner, sub = slot // per_owner, slot % per_owner
        if group_size <= per_owner:
            holder, local = sub // per, owner * per + sub % per
        else:
            holder, local = sub + per_owner * (owner % (group_size // per_owner)), owner
        here = jnp.logical_and(valid, jnp.logical_and(~is_own, holder == position))
        far_list[mine] = pack(first, local, offset)
        spare[own] = pack(first, jnp.clip(code, 0, own_count - 1), offset)
        tally[holder] = tally[holder] + jnp.where(jnp.logical_and(valid, ~is_own), 1, 0)
        return mine + jnp.where(here, 1, 0), own + jnp.where(is_own, 1, 0)

    state = (jnp.int32(0), jnp.int32(0))
    for g in range(group_size):
        state = lax.fori_loop(0, counts[g], functools.partial(scan, g), state)
    mine, own = state
    everything = own
    for g in range(group_size):
        everything = everything + tally[g]
    share = (everything + group_size - 1) // group_size
    begin = jnp.int32(0)
    for g in range(group_size):
        begin = begin + jnp.where(g < position, jnp.maximum(share - tally[g], 0), 0)
    stop = jnp.minimum(begin + jnp.maximum(share - mine, 0), own)
    begin = jnp.minimum(begin, own)

    def take(i, carry):
        own_list[i - begin] = spare[i]
        return carry

    lax.fori_loop(begin, stop, take, 0)
    for i in range(batch):
        far_list[mine + i] = pack(own_count, slots, 0)
        own_list[stop - begin + i] = pack(own_count, own_count, 0)
    totals[0] = mine
    totals[1] = stop - begin


def pair_kernel(
    far, own_count, extent, width, pad, listed, totals, own_full, other, plane, first_block,
    scale, *rest,
):
    if far:
        own_out, far_out, firsts, seconds, first_sums, second_sums, density, middle, field = rest
    else:
        own_out, firsts, seconds, first_sums, second_sums, density, middle, field = rest
    chunks = width // lanes
    tall = extent + 2 * pad
    second_count = seconds.shape[0] - 1
    inner = slice(pad, pad + extent)
    zeros = jnp.zeros((chunks, tall, lanes), jnp.float32)
    edge = jnp.zeros((chunks, pad, lanes), jnp.float32)

    def part(s):
        return slice(s * lanes, (s + 1) * lanes)

    def fill_own(n, carry):
        for s in range(chunks):
            box = own_full[n, :, part(s)].astype(jnp.float32)
            firsts[n, s] = box
            if far:
                first_sums[n, s] = jnp.zeros_like(box)
            else:
                seconds[n, s, inner] = box
                first_sums[n, s] = other[n, :, part(s)]
        return carry

    def fill_far(n, carry):
        group_size, per, rows = other.shape[1:4]
        for h in range(group_size):
            for s in range(chunks):
                seconds[n, s, pad + h * rows : pad + (h + 1) * rows] = other[
                    n // per, h, n % per, :, part(s)
                ].astype(jnp.float32)
        return carry

    def clear(n, carry):
        seconds[n, :, :pad] = edge
        seconds[n, :, pad + extent :] = edge
        second_sums[n] = zeros
        return carry

    lax.fori_loop(0, second_count, clear, 0)
    lax.fori_loop(0, own_count, fill_own, 0)
    if far:
        lax.fori_loop(0, second_count, fill_far, 0)
    firsts[own_count] = jnp.zeros((chunks, extent, lanes), jnp.float32)
    first_sums[own_count] = jnp.zeros((chunks, extent, lanes), jnp.float32)
    seconds[second_count] = zeros
    second_sums[second_count] = zeros

    def unpack(turn, b):
        word = listed[turn * batch + b]
        return word % 256, (word // 256) % 256, 2 * pad - word // 65536

    step = 256
    some = 4 if chunks % 4 == 0 else 1

    def turn_body(turn, carry):
        for b in range(batch):
            first, second, start = unpack(turn, b)
            rows = slice(b * extent, (b + 1) * extent)
            for s in range(chunks):
                moved = seconds[second, s, pl.ds(start, extent), :]
                density[rows, part(s)] = (firsts[first, s] * moved).astype(jnp.bfloat16)
        for n in range(width // step):
            columns = slice(n * step, (n + 1) * step)
            wave = jnp.dot(density[...], plane[:, columns], preferred_element_type=jnp.float32)
            wave = jnp.dot(
                first_block[...], wave.astype(jnp.bfloat16), preferred_element_type=jnp.float32
            )
            wave = wave.reshape(batch, extent, step) * scale[:, columns][None]
            wave = wave.reshape(batch * extent, step).astype(jnp.bfloat16)
            wave = jnp.dot(first_block[...], wave, preferred_element_type=jnp.float32)
            middle[:, columns] = wave.astype(jnp.bfloat16)
        for n in range(width // step):
            columns = slice(n * step, (n + 1) * step)
            field[:, columns] = jnp.dot(
                middle[...], plane[:, columns], preferred_element_type=jnp.float32
            )
        for b in range(batch):
            first, second, start = unpack(turn, b)
            rows = slice(b * extent, (b + 1) * extent)
            window = pl.ds(start, extent)
            for q in range(0, chunks, some):
                group = range(q, q + some)
                firsts_were = [first_sums[first, s] for s in group]
                seconds_were = [second_sums[second, s, window, :] for s in group]
                values = [field[rows, part(s)] for s in group]
                for k, s in enumerate(group):
                    first_sums[first, s] = (
                        firsts_were[k] + values[k] * seconds[second, s, window, :]
                    )
                for k, s in enumerate(group):
                    second_sums[second, s, window, :] = (
                        seconds_were[k] + values[k] * firsts[first, s]
                    )
        return carry

    lax.fori_loop(0, (totals[0 if far else 1] + batch - 1) // batch, turn_body, 0)

    def give_own(n, carry):
        for s in range(chunks):
            value = first_sums[n, s]
            if not far:
                value = value + second_sums[n, s, inner]
            own_out[n, :, part(s)] = value.astype(own_out.dtype)
        return carry

    def give_far(n, carry):
        group_size, per, rows = far_out.shape[1:4]
        for h in range(group_size):
            for s in range(chunks):
                far_out[n // per, h, n % per, :, part(s)] = second_sums[
                    n, s, pad + h * rows : pad + (h + 1) * rows
                ].astype(far_out.dtype)
        return carry

    lax.fori_loop(0, own_count, give_own, 0)
    if far:
        lax.fori_loop(0, second_count, give_far, 0)


def join_kernel(local, own, returned, out):
    out[...] = own[...].astype(jnp.float32)

    def add(n, carry):
        out[local[n]] += returned[n].astype(jnp.float32)
        return carry

    lax.fori_loop(0, returned.shape[0], add, 0)


def shards(orbitals, anchors, wanted, pairs, counts):
    group_size = lax.axis_size("grp")
    member = lax.axis_index("orb")
    position = lax.axis_index("grp")
    own_count, rows, width = orbitals.shape
    extent = rows * group_size
    pad = extent // 4
    owners, per_owner = wanted.shape[0], wanted.shape[2]
    per = -(-per_owner // group_size)
    slots = owners * per
    capacity = pairs.shape[2]
    smem = pl.BlockSpec(memory_space=pltpu.SMEM)
    vmem = pl.BlockSpec(memory_space=pltpu.VMEM)

    slab = orbitals.astype(jnp.bfloat16)
    own_full = lax.all_gather(slab, "grp", axis=1, tiled=True)

    send_ids = lax.dynamic_index_in_dim(wanted, member, 1, keepdims=False)
    request = lax.dynamic_index_in_dim(wanted, member, 0, keepdims=False).reshape(-1)
    if group_size <= per_owner:
        room = per * group_size - per_owner
        send_ids = jnp.pad(send_ids, ((0, 0), (0, room)), constant_values=-1)
    else:
        send_ids = jnp.tile(send_ids, (1, -(-group_size // per_owner)))[:, :group_size]
    send_ids = send_ids.reshape(-1)
    send_local = jnp.where(send_ids >= 0, send_ids - member * own_count, 0)
    outgoing = slab[send_local]
    arrived = lax.all_to_all(outgoing, ("orb", "grp"), split_axis=0, concat_axis=0, tiled=True)
    arrived = arrived.reshape(owners, group_size, per, rows, width)

    sine_rows = sine_table(extent)
    plane = jnp.kron(sine_rows, sine_rows)
    first_block = jnp.kron(jnp.eye(batch, dtype=jnp.bfloat16), sine_rows)
    scale = (1.0 / denominator(extent)).reshape(extent, width)

    size = group_size * capacity + 2 * batch
    sizes = (group_size, capacity, own_count, per_owner, per, slots, pad)
    words = jax.ShapeDtypeStruct((size,), jnp.int32)
    far_list, own_list, totals = pl.pallas_call(
        functools.partial(list_kernel, sizes),
        out_shape=(words, words, jax.ShapeDtypeStruct((2,), jnp.int32)),
        in_specs=[smem] * 5,
        out_specs=(smem, smem, smem),
        scratch_shapes=[pltpu.SMEM((size,), jnp.int32), pltpu.SMEM((group_size,), jnp.int32)],
    )(
        jnp.stack([member, position]).astype(jnp.int32),
        pairs.reshape(-1),
        counts.reshape(-1),
        anchors,
        request,
    )

    tall = extent + 2 * pad
    chunks = width // lanes

    def run(far, listed, other, out_shape):
        count = slots if far else own_count
        return pl.pallas_call(
            functools.partial(pair_kernel, far, own_count, extent, width, pad),
            out_shape=out_shape,
            in_specs=[smem, smem] + [vmem] * 5,
            out_specs=(vmem,) * len(out_shape),
            scratch_shapes=[
                pltpu.VMEM((own_count + 1, chunks, extent, lanes), jnp.float32),
                pltpu.VMEM((count + 1, chunks, tall, lanes), jnp.float32),
                pltpu.VMEM((own_count + 1, chunks, extent, lanes), jnp.float32),
                pltpu.VMEM((count + 1, chunks, tall, lanes), jnp.float32),
                pltpu.VMEM((batch * extent, width), jnp.bfloat16),
                pltpu.VMEM((batch * extent, width), jnp.bfloat16),
                pltpu.VMEM((batch * extent, width), jnp.float32),
            ],
            cost_estimate=pl.CostEstimate(
                flops=60_000_000_000, bytes_accessed=16_000_000, transcendentals=0
            ),
            compiler_params=pltpu.CompilerParams(vmem_limit_bytes=52 * 2**20),
        )(listed, totals, own_full, other, plane, first_block, scale)

    whole = (own_count, extent, width)
    own_part, far_sum = run(
        True,
        far_list,
        arrived,
        (
            jax.ShapeDtypeStruct(whole, jnp.float32),
            jax.ShapeDtypeStruct(arrived.shape, jnp.bfloat16),
        ),
    )
    returned = lax.all_to_all(
        far_sum.reshape(-1, rows, width), ("orb", "grp"), split_axis=0, concat_axis=0, tiled=True
    )
    (own_sum,) = run(False, own_list, own_part, (jax.ShapeDtypeStruct(whole, jnp.bfloat16),))
    own_mine = lax.psum_scatter(own_sum, "grp", scatter_dimension=1, tiled=True)
    return pl.pallas_call(
        join_kernel,
        out_shape=jax.ShapeDtypeStruct((own_count, rows, width), jnp.float32),
        in_specs=[smem, vmem, vmem],
        out_specs=vmem,
        compiler_params=pltpu.CompilerParams(vmem_limit_bytes=40 * 2**20),
    )(send_local, own_mine, returned)


def solution(mesh):
    return jax.shard_map(
        shards,
        mesh=mesh,
        in_specs=(P("orb", "grp", None), P(), P(), P("orb", None, None, None), P("orb", None)),
        out_specs=P("orb", "grp", None),
        check_vma=False,
    )
```

time: 243 us -> 199 us (0.82)
  blocking collectives: 30.9 us -> 0 us
  waiting for transfers between devices: 65.3 us -> 44.6 us
  starting transfers between devices: 5.66 us -> 14.2 us
  other arithmetic: 11.5 us -> 8.08 us
  Pallas kernels: 94.1 us -> 97 us
    all_to_all x1 -> x0, blocking collectives: 30.9 us -> none  [shards(): lax.all_to_all(far_sum, 'orb', split_axis=0, concat_axis=0, tiled=True)]
    all_gather x1, waiting for transfers between devices: 33.8 us -> 6.69 us  [shards(): own_full = lax.all_gather(slab, 'grp', axis=1, tiled=True)]
    all_to_all x1 -> x2, waiting for transfers between devices: 0.01 us -> 26.2 us  [the longest x1 26.1 us: shards(): lax.all_to_all(far_sum.reshape(-1, rows, width), ('orb', 'grp'), split_ax...]
    reduce_scatter x1, waiting for transfers between devices: 31.4 us -> 11.7 us  [shards(): own_mine = lax.psum_scatter(own_sum, 'grp', scatter_dimension=1, tiled=True)]
    all_to_all x1 -> x2, starting transfers between devices: 5.61 us -> 14.1 us  [the longest x1 7.3 us: shards(): lax.all_to_all(outgoing, ('orb', 'grp'), split_axis=0, concat_axis=0, til...]
    pallas_call x3 -> x4, Pallas kernels: 94.1 us -> 97 us  [the longest x2 84.8 us: run(): pl.pallas_call(functools.partial(pair_kernel, far, own_count, extent, wid...]
    convert_element_type x2 -> x1, other arithmetic: 5.55 us -> 2.78 us  [shards(): slab = orbitals.astype(jnp.bfloat16)]
  transfers between devices with their start and end apart: 3 -> 4, of which waited for: 2 -> 3; matrix products, arithmetic and copies ran while one was open for 9% -> 12% of each run, Pallas kernels for 4% -> 5%
where the time goes in v2:
time: 199 us; the launch traced here: 198 us
  Pallas kernels  97 us (49%)
  waiting for transfers between devices  44.6 us (22%)
  local copies, waits for them, and re-layouts  20.5 us (10%)
  starting transfers between devices  14.2 us (7%)
  between operations  13.6 us (7%)
  other arithmetic  8.08 us (4%)
    pallas_call x2, Pallas kernels, run(): pl.pallas_call(functools.partial(pair_kernel, far, own_count, extent, wid...  84.8 us
    all_to_all x1, waiting for transfers between devices, shards(): lax.all_to_all(far_sum.reshape(-1, rows, width), ('orb', 'grp'), split_ax...  26.1 us
    mul x1, local copies, waits for them, and re-layouts, shards(): plane = jnp.kron(sine_rows, sine_rows)  12.4 us
    reduce_scatter x1, waiting for transfers between devices, shards(): own_mine = lax.psum_scatter(own_sum, 'grp', scatter_dimension=1, tiled=True)  11.7 us
    pallas_call x1, Pallas kernels, shards(): pl.pallas_call(functools.partial(list_kernel, sizes), out_shape=(words, w...  9.87 us
    all_to_all x1, starting transfers between devices, shards(): lax.all_to_all(outgoing, ('orb', 'grp'), split_axis=0, concat_axis=0, til...  7.3 us
    all_to_all x1, starting transfers between devices, shards(): lax.all_to_all(far_sum.reshape(-1, rows, width), ('orb', 'grp'), split_ax...  6.82 us
    all_gather x1, waiting for transfers between devices, shards(): own_full = lax.all_gather(slab, 'grp', axis=1, tiled=True)  6.69 us
  transfers between devices with their start and end apart: 4, of which 3 were waited for; matrix products, arithmetic and copies ran while one was open for 12% of the time, Pallas kernels for 5%

profile of v2, /device:TPU:0, one launch (start us, length us, event | category | flops | bytes accessed | tf_op | source)
XLA Modules:
  0.0 198.0 jit_solution(2872429938653910091)
XLA Ops:
  6.5 2.8 %convert_element_type.29 = bf16[32,16,1024]{2,1,0:T(8,128)(2,1)} convert(f32[32,16,1024]{2,1,0:T(8,128)} %param.5) | non-fusion elementwise | flops 524288 | bytes 3145728 | tf_op jit(solution)/shard_map/convert_element_type | solution.py:242
  9.4 0.4 fusion
  9.8 0.1 select_n.27
  9.9 2.8 %gather_fusion = bf16[32,16,1024]{2,1,0:T(8,128)(2,1)} fusion(bf16[32,16,1024]{2,1,0:T(8,128)(2,1)} %convert_element_type.29, s32[1024]{0:T(1024)S(1)} %pad_clamp_fusion), kind=kCustom, calls=%fused_computation | custom fusion | bytes 2097280 | tf_op jit(solution)/shard_map/gather | solution.py:254
  12.7 7.3 %all-to-all-start = ((bf16[32,16,1024]{2,1,0:T(8,128)(2,1)}), bf16[32,16,1024]{2,1,0:T(8,128)(2,1)S(1)}, u32[]{:S(2)}, u32[]{:S(2)}) async-start(bf16[32,16,1024]{2,1,0:T(8,128)(2,1)} %gather_fusion), calls=%async_computation | async-start | bytes 2097152 | tf_op jit(solution)/shard_map/all_to_all | solution.py:255
  20.0 0.0 reduce-scatter.2.cloned.1.call-start
  20.1 0.1 copy.9
  20.2 0.7 reshape.210.request
  20.9 0.1 copy.8
  21.0 0.7 reshape.208.pairs
  21.8 0.1 multiply_convert_fusion
  21.9 3.8 %broadcast_multiply_fusion = bf16[32,32,32,32]{3,2,1,0:T(8,128)(2,1)} fusion(bf16[32,32]{1,0:T(8,128)(2,1)S(1)} %multiply_convert_fusion), kind=kLoop, calls=%fused_computation.1 | loop fusion | flops 1048576 | bytes 2099200 | tf_op jit(solution)/shard_map/jit(kron)/mul | solution.py:259
  25.8 12.4 %mul.179.plane = bf16[1024,1024]{1,0:T(8,128)(2,1)} reshape(bf16[32,32,32,32]{3,2,1,0:T(8,128)(2,1)} %broadcast_multiply_fusion) | data formatting | bytes 4194304 | tf_op jit(solution)/shard_map/jit(kron)/mul | solution.py:259
  38.2 0.1 broadcast_multiply_fusion.1
  38.3 0.4 mul.183.first_block
  38.7 0.1 broadcast_add_fusion
  38.8 0.2 add.123
  39.0 0.2 add.124
  39.2 0.1 add.125
  39.3 0.6 pad_add_fusion.where
  39.9 9.9 %shard_map.55 = (s32[496]{0:T(512)}, s32[496]{0:T(512)}, s32[2]{0:T(128)}) custom-call(s32[2]{0:T(128)} %pad_add_fusion.where, s32[960]{0:T(1024)} %reshape.208.pairs, s32[2]{0:T(128)} %bitcast.16, s32[512]{0:T(512)} %anchors.1, s32[32]{0:T(128)} %reshape.210.request), custom_call_target="tpu_custom_call" | custom-call | tf_op jit(solution)/shard_map/pallas_call | solution.py:266
  49.9 6.7 %all-gather.2.cloned.1.call-done.own_full = bf16[32,32,1024]{2,1,0:T(8,128)(2,1)} async-done(((bf16[32,16,1024]{2,1,0:T(8,128)(2,1)}), bf16[32,32,1024]{2,1,0:T(8,128)(2,1)}) %all-gather.2.cloned.1.call-update) | async-done | bytes 2097168 | tf_op jit(solution)/shard_map/all_gather | solution.py:243
  56.6 0.7 copy-done.2
  57.2 0.7 copy-done.3
  57.9 52.9 %shard_map.56 = (f32[32,32,1024]{2,1,0:T(8,128)}, bf16[16,2,1,16,1024]{4,3,2,1,0:T(8,128)(2,1)}) custom-call(s32[496]{0:T(512)S(1)} %copy-done.2, s32[2]{0:T(128)S(1)} %copy-done.3, bf16[32,32,1024]{2,1,0:T(8,128)(2,1)} %all-gather.2.cloned.1.call-done.own_full, bf16[16,2,1,16,1024]{4,3,2,1,0:T(8,128)(2,1)} %bitcast.15, bf16[1024,1024]{1,0:T(8,128)(2,1)} %mul.179.plane, ...), custom_call_target="tpu_custom_call" | custom-call | flops 60000002048 | bytes 16000000 | tf_op jit(solution)/shard_map/pallas_call | solution.py:285
  110.8 32.0 %shard_map.57 = bf16[32,32,1024]{2,1,0:T(8,128)(2,1)} custom-call(s32[496]{0:T(512)S(1)} %copy-done.1, s32[2]{0:T(128)S(1)} %copy-done.3, bf16[32,32,1024]{2,1,0:T(8,128)(2,1)} %all-gather.2.cloned.1.call-done.own_full, f32[32,32,1024]{2,1,0:T(8,128)} %get-tuple-element.13.other, bf16[1024,1024]{1,0:T(8,128)(2,1)} %mul.179.plane, ...), custom_call_target="tpu_custom_call" | custom-call | flops 60000002048 | bytes 16000000 | tf_op jit(solution)/shard_map/pallas_call | solution.py:285
  142.8 6.8 %all-to-all-start.1 = ((bf16[32,16,1024]{2,1,0:T(8,128)(2,1)}), bf16[32,16,1024]{2,1,0:T(8,128)(2,1)S(1)}, u32[]{:S(2)}, u32[]{:S(2)}) async-start(bf16[32,16,1024]{2,1,0:T(8,128)(2,1)} %bitcast.6), calls=%async_computation.2 | async-start | bytes 2097152 | tf_op jit(solution)/shard_map/all_to_all | solution.py:315
  149.6 0.1 select_n.26.local
  149.7 26.1 %all-to-all-done.1.returned = bf16[32,16,1024]{2,1,0:T(8,128)(2,1)S(1)} async-done(((bf16[32,16,1024]{2,1,0:T(8,128)(2,1)}), bf16[32,16,1024]{2,1,0:T(8,128)(2,1)S(1)}, u32[]{:S(2)}, u32[]{:S(2)}) %all-to-all-start.1) | async-done | bytes 1048608 | tf_op jit(solution)/shard_map/all_to_all | solution.py:315
  175.8 11.7 %reduce-scatter.2.cloned.1.call-done.own = bf16[32,16,1024]{2,1,0:T(8,128)(2,1)} async-done(((bf16[32,32,1024]{2,1,0:T(8,128)(2,1)}), bf16[32,16,1024]{2,1,0:T(8,128)(2,1)}) %reduce-scatter.2.cloned.1.call-update) | async-done | bytes 1048592 | tf_op jit(solution)/shard_map/reduce_scatter | solution.py:319
  187.6 1.2 copy-done
  188.8 2.3 %shard_map.58 = f32[32,16,1024]{2,1,0:T(8,128)} custom-call(s32[32]{0:T(128)S(1)} %select_n.26.local, bf16[32,16,1024]{2,1,0:T(8,128)(2,1)S(1)} %copy-done, bf16[32,16,1024]{2,1,0:T(8,128)(2,1)S(1)} %all-to-all-done.1.returned), custom_call_target="tpu_custom_call" | custom-call | tf_op jit(solution)/shard_map/pallas_call | solution.py:320
  (23 shorter events, 0.2 us)
Async XLA Ops:
  6.5 2.8 %copy-start.5 = (s32[16,16,2]{1,2,0:T(2,128)S(1)}, s32[16,16,2]{1,2,0:T(2,128)}, u32[]{:S(2)}) copy-start(s32[16,16,2]{1,2,0:T(2,128)} %param.7) | copy-start | bytes 6148
  6.5 14.4 %copy-start.6 = (s32[1,2,240,2]{2,3,1,0:T(2,128)S(1)}, s32[1,2,240,2]{2,3,1,0:T(2,128)}, u32[]{:S(2)}) copy-start(s32[1,2,240,2]{2,3,1,0:T(2,128)} %param.8) | copy-start | bytes 11524
  6.5 50.0 %all-gather.2.cloned.1.call-start = ((), (), s32[]{:S(2)}) async-start(), calls=%async_computation.3 | async-start | bytes 3145728 | tf_op jit(solution)/shard_map/all_gather | solution.py:243
  12.7 37.1 %all-to-all-start = ((bf16[32,16,1024]{2,1,0:T(8,128)(2,1)}), bf16[32,16,1024]{2,1,0:T(8,128)(2,1)S(1)}, u32[]{:S(2)}, u32[]{:S(2)}) async-start(bf16[32,16,1024]{2,1,0:T(8,128)(2,1)} %gather_fusion), calls=%async_computation | async-start | bytes 2097152 | tf_op jit(solution)/shard_map/all_to_all | solution.py:255
  20.0 167.5 %reduce-scatter.2.cloned.1.call-start = ((), (), s32[]{:S(2)}) async-start(), calls=%async_computation.4 | async-start | bytes 3145728 | tf_op jit(solution)/shard_map/reduce_scatter | solution.py:319
  49.9 6.7 %copy-start.4 = (bf16[32,16,1024]{2,1,0:T(8,128)(2,1)}, bf16[32,16,1024]{2,1,0:T(8,128)(2,1)S(1)}, u32[]{:S(2)}) copy-start(bf16[32,16,1024]{2,1,0:T(8,128)(2,1)S(1)} %all-to-all-done) | copy-start | bytes 3145732
  56.6 0.7 copy-start.2
  57.2 0.7 copy-start.3
  57.9 52.9 %copy-start.1 = (s32[496]{0:T(512)S(1)}, s32[496]{0:T(512)}, u32[]{:S(2)}) copy-start(s32[496]{0:T(512)} %get-tuple-element.10.listed) | copy-start | bytes 5956
  142.8 33.1 %all-to-all-start.1 = ((bf16[32,16,1024]{2,1,0:T(8,128)(2,1)}), bf16[32,16,1024]{2,1,0:T(8,128)(2,1)S(1)}, u32[]{:S(2)}, u32[]{:S(2)}) async-start(bf16[32,16,1024]{2,1,0:T(8,128)(2,1)} %bitcast.6), calls=%async_computation.2 | async-start | bytes 2097152 | tf_op jit(solution)/shard_map/all_to_all | solution.py:315
  187.6 1.2 copy-start
Sparse Core Ops, SparseCore 0:
  9.5 47.0 all-gather.1
  142.9 44.6 reduce-scatter.1
